TPU v7x, 128 devices: a whole 4x4x4 slice. The times are simulated.
128 devices in a mesh: dp: 8 (over x_hi, z), tensor: 16 (over x_lo, y, core).
Axes of the slice: x: 4 (x_hi: 2, x_lo: 2; x = x_hi * 2 + x_lo), y: 4, z: 4, core: 2. Of those that a mesh axis runs over, the one named last changes fastest.
Arguments:
- history: bfloat16 [17, 16384, 2048], P(None, ('dp', 'tensor')), may hold values from -6 to 6
- cotangent: bfloat16 [16384, 2048], P(('dp', 'tensor')), may hold values from -6 to 6
- lengths: int32 [8, 4], replicated, may hold values from 0 to 2048, as said below
- mix_gain: float32 [2048], replicated, may hold values from 0.5 to 1.5
- mix_first: float32 [2048, 68], replicated, may hold values from -0.125 to 0.125
- mix_second: float32 [68, 68], replicated, may hold values from -0.3 to 0.3
- mix_bias: float32 [68], replicated, may hold values from -1.8 to 1.8
- gain_query: float32 [2048], replicated, may hold values from 0.5 to 1.5
- gain_key: float32 [2048], replicated, may hold values from 0.5 to 1.5
- gain_value: float32 [2048], replicated, may hold values from 0.5 to 1.5
- gain_mlp: float32 [2048], replicated, may hold values from 0.5 to 1.5
- w_query: bfloat16 [2048, 2048], P(None, 'tensor'), may hold values from -0.125 to 0.125
- w_key: bfloat16 [2048, 2048], P(None, 'tensor'), may hold values from -0.125 to 0.125
- w_value: bfloat16 [2048, 2048], P(None, 'tensor'), may hold values from -0.125 to 0.125
- w_output: bfloat16 [2048, 2048], P('tensor'), may hold values from -1 to 1
- w_expand: bfloat16 [2048, 8192], P(None, 'tensor'), may hold values from -0.125 to 0.125
- w_reduce: bfloat16 [8192, 2048], P('tensor'), may hold values from -0.0625 to 0.0625
Outputs:
- output: bfloat16 [16384, 2048], P(('dp', 'tensor'))
- grad_history: bfloat16 [17, 16384, 2048], P(None, ('dp', 'tensor'))
- grad_mix_gain: float32 [2048], replicated
- grad_mix_first: float32 [2048, 68], replicated
- grad_mix_second: float32 [68, 68], replicated
- grad_mix_bias: float32 [68], replicated
- grad_gain_query: float32 [2048], replicated
- grad_gain_key: float32 [2048], replicated
- grad_gain_value: float32 [2048], replicated
- grad_gain_mlp: float32 [2048], replicated
- grad_w_query: float32 [2048, 2048], P('dp', 'tensor')
- grad_w_key: float32 [2048, 2048], P('dp', 'tensor')
- grad_w_value: float32 [2048, 2048], P('dp', 'tensor')
- grad_w_output: float32 [2048, 2048], P('tensor', 'dp')
- grad_w_expand: float32 [2048, 8192], P('dp', 'tensor')
- grad_w_reduce: float32 [8192, 2048], P('tensor', 'dp')
Inputs may be any that keep to these rules, and one draw needn't show every extreme that they name: Row g holds, in order, the lengths of the sequences packed into the 2048 tokens of data index g (0 marks an empty slot); each row sums to 2048, its longest entry is 1024 or more, and in some row one sequence fills all 2048 tokens.
All inputs are finite; a program needn't handle non-finite values.
Results may differ from a plain program's by a relative error of at most 0.019.
Values may be sent and summed in bfloat16 or wider, within the bound.
A program may use at most 320 MiB of HBM per device.

v0:
```python
import jax
import jax.numpy as jnp
from jax import lax
from jax.sharding import PartitionSpec as P

HEAD_DIM = 128
HISTORY = 17
STREAMS = 4
NORM_EPS = 1e-06
MASKED = -1e30
PRECISE = lax.Precision.HIGHEST


def swapped(x, axis, bit):
    return lax.ppermute(x, axis, [(i, i ^ 1 << bit) for i in range(lax.axis_size(axis))])


def rms_scale(values, gain_vector):
    inverse = lax.rsqrt(jnp.mean(values * values, axis=-1, keepdims=True) + NORM_EPS)
    return values * inverse * gain_vector


def matmul(left_side, right_side):
    return jnp.dot(left_side, right_side, precision=PRECISE)


def front_part(
    history_float, mix_gain, mix_first, mix_second, mix_bias, gain_query, gain_key, gain_value
):
    latest = rms_scale(history_float[HISTORY - 1], mix_gain)
    hidden = jax.nn.gelu(matmul(latest, mix_first), approximate=False)
    mixing = (matmul(hidden, mix_second) + mix_bias).reshape(
        history_float.shape[1], STREAMS, HISTORY
    )
    streams = jnp.einsum("tkj,jtd->ktd", mixing, history_float, precision=PRECISE)
    return (
        rms_scale(streams[0], gain_query),
        rms_scale(streams[1], gain_key),
        rms_scale(streams[2], gain_value),
        streams[3],
    )


def gelu_exact(values):
    return jax.nn.gelu(values, approximate=False)


def across_rows(left_side, right_side):
    return lax.dot_general(
        left_side, right_side, (((0,), (0,)), ((), ())), preferred_element_type=jnp.float32
    )


def across_cols(left_side, right_side):
    return lax.dot_general(
        left_side, right_side, (((1,), (1,)), ((), ())), preferred_element_type=jnp.float32
    )


def segment_of(places, doc_ends):
    return jnp.sum((places[:, None] >= doc_ends[None, :]).astype(jnp.int32), axis=1)


def gather_bits(piece, bit_list, join_dim, device_index):
    for bit_number in bit_list:
        partner = swapped(piece, "tensor", bit_number)
        upper = device_index // (1 << bit_number) % 2 == 1
        piece = jnp.where(
            upper,
            jnp.concatenate([partner, piece], axis=join_dim),
            jnp.concatenate([piece, partner], axis=join_dim),
        )
    return piece


def sum_bits(partial_value, bit_list, device_index, split_dim):
    for bit_number in reversed(bit_list):
        half_size = partial_value.shape[split_dim] // 2
        lower_half = lax.slice_in_dim(partial_value, 0, half_size, axis=split_dim)
        upper_half = lax.slice_in_dim(partial_value, half_size, 2 * half_size, axis=split_dim)
        upper = device_index // (1 << bit_number) % 2 == 1
        keep_half = jnp.where(upper, upper_half, lower_half)
        send_half = jnp.where(upper, lower_half, upper_half)
        partial_value = keep_half + swapped(
            send_half.astype(jnp.bfloat16), "tensor", bit_number
        ).astype(send_half.dtype)
    return partial_value


def make_scores(query_heads, key_heads, query_places, key_places, doc_ends):
    block_rows = min(512, query_heads.shape[0])
    scale_factor = HEAD_DIM ** (-0.5)
    query_segments = segment_of(query_places, doc_ends)
    key_segments = segment_of(key_places, doc_ends)

    def block_scores(block_index):
        scores = (
            jnp.einsum("qhd,khd->hqk", query_heads, key_heads, preferred_element_type=jnp.float32)
            * scale_factor
        )
        allowed = (query_places[:, None] >= key_places[None, :]) & (
            query_segments[:, None] == key_segments[None, :]
        )
        return (jnp.where(allowed[None], scores, MASKED), query_heads)

    return (block_scores, block_rows)


def on_device(
    history,
    cotangent,
    lengths,
    mix_gain,
    mix_first,
    mix_second,
    mix_bias,
    gain_query,
    gain_key,
    gain_value,
    gain_mlp,
    w_query,
    w_key,
    w_value,
    w_output,
    w_expand,
    w_reduce,
):
    shard_rows = history.shape[1]
    tensor_size = lax.axis_size("tensor")
    tok_group = shard_rows * tensor_size
    model_width = w_query.shape[0]
    tensor_index = lax.axis_index("tensor")
    low_bits = [0, 1]
    high_bits = list(range(2, tensor_size.bit_length() - 1))
    scale_factor = HEAD_DIM ** (-0.5)
    history_float = history.astype(jnp.float32)
    front_values, front_back = jax.vjp(
        front_part,
        history_float,
        mix_gain,
        mix_first,
        mix_second,
        mix_bias,
        gain_query,
        gain_key,
        gain_value,
    )
    query_norm, key_norm, value_norm, residual = front_values
    query_low = query_norm.astype(jnp.bfloat16)
    key_low = key_norm.astype(jnp.bfloat16)
    value_low = value_norm.astype(jnp.bfloat16)
    length_row = lax.dynamic_index_in_dim(lengths, lax.axis_index("dp"), 0, keepdims=False)
    doc_ends = jnp.cumsum(length_row)
    query_rows = gather_bits(query_low, high_bits, 0, tensor_index)
    key_rows = gather_bits(key_low, high_bits, 0, tensor_index)
    value_rows = gather_bits(value_low, high_bits, 0, tensor_index)
    cot_rows = gather_bits(cotangent, high_bits, 0, tensor_index)
    query_whole = gather_bits(w_query, low_bits, 1, tensor_index)
    key_whole = gather_bits(w_key, low_bits, 1, tensor_index)
    value_whole = gather_bits(w_value, low_bits, 1, tensor_index)
    output_whole = gather_bits(w_output, low_bits, 0, tensor_index)
    expand_whole = gather_bits(w_expand, low_bits, 1, tensor_index)
    reduce_whole = gather_bits(w_reduce, low_bits, 0, tensor_index)
    group_count = tensor_size // 4
    part_index = tensor_index % 4
    inner_rows = jnp.arange(shard_rows, dtype=jnp.int32)
    group_offsets = 4 * jnp.arange(group_count, dtype=jnp.int32)
    query_places = (
        (part_index + group_offsets)[:, None] * shard_rows + inner_rows[None, :]
    ).reshape(-1)
    key_places = (
        (jnp.arange(4, dtype=jnp.int32)[:, None, None] + group_offsets[None, :, None]) * shard_rows
        + inner_rows[None, None, :]
    ).reshape(-1)
    row_count = query_rows.shape[0]
    heads_here = query_whole.shape[1] // HEAD_DIM
    query_heads = (
        jnp.dot(query_rows, query_whole, preferred_element_type=jnp.float32)
        .astype(jnp.bfloat16)
        .reshape(row_count, heads_here, HEAD_DIM)
    )
    key_part = jnp.dot(key_rows, key_whole, preferred_element_type=jnp.float32).astype(jnp.bfloat16)
    value_part = jnp.dot(value_rows, value_whole, preferred_element_type=jnp.float32).astype(
        jnp.bfloat16
    )
    key_flat = gather_bits(key_part, low_bits, 0, tensor_index)
    value_flat = gather_bits(value_part, low_bits, 0, tensor_index)
    key_heads = key_flat.reshape(tok_group, heads_here, HEAD_DIM)
    value_heads = value_flat.reshape(tok_group, heads_here, HEAD_DIM)
    block_scores, block_rows = make_scores(
        query_heads, key_heads, query_places, key_places, doc_ends
    )
    block_count = row_count // block_rows

    def forward_block(block_index):
        masked, query_block = block_scores(block_index)
        top_score = jnp.max(masked, axis=-1, keepdims=True)
        exponent = jnp.exp(masked - top_score)
        row_total = jnp.sum(exponent, axis=-1, keepdims=True)
        weights_low = (exponent / row_total).astype(jnp.bfloat16)
        context_block = jnp.einsum(
            "hqk,khd->qhd", weights_low, value_heads, preferred_element_type=jnp.float32
        )
        return (context_block, top_score + jnp.log(row_total))

    context_blocks, log_totals = lax.map(forward_block, jnp.arange(block_count))
    context = context_blocks.reshape(row_count, heads_here * HEAD_DIM).astype(jnp.bfloat16)
    attended = sum_bits(
        jnp.dot(context, output_whole, preferred_element_type=jnp.float32),
        high_bits,
        tensor_index,
        0,
    )
    middle = residual + attended
    mlp_norm, norm_back = jax.vjp(rms_scale, middle, gain_mlp)
    mlp_low = mlp_norm.astype(jnp.bfloat16)
    mlp_gathered = gather_bits(mlp_low, high_bits, 0, tensor_index)
    expanded = jnp.dot(mlp_gathered, expand_whole, preferred_element_type=jnp.float32)
    activated, gelu_back = jax.vjp(gelu_exact, expanded)
    active_low = activated.astype(jnp.bfloat16)
    reduced = sum_bits(
        jnp.dot(active_low, reduce_whole, preferred_element_type=jnp.float32),
        high_bits,
        tensor_index,
        0,
    )
    output = (middle + reduced).astype(jnp.bfloat16)
    grad_w_reduce = across_rows(active_low, cot_rows)
    grad_active = across_cols(cot_rows, reduce_whole)
    (grad_expanded,) = gelu_back(grad_active)
    expand_low = grad_expanded.astype(jnp.bfloat16)
    grad_w_expand = across_rows(mlp_gathered, expand_low)
    grad_mlp_norm = sum_bits(across_cols(expand_low, expand_whole), high_bits, tensor_index, 0)
    grad_w_expand = sum_bits(grad_w_expand, low_bits, tensor_index, 1)
    grad_w_reduce = sum_bits(grad_w_reduce, low_bits, tensor_index, 0)
    grad_middle_norm, grad_gain_mlp = norm_back(grad_mlp_norm)
    grad_middle = cotangent.astype(jnp.float32) + grad_middle_norm
    middle_low = grad_middle.astype(jnp.bfloat16)
    middle_rows = gather_bits(middle_low, high_bits, 0, tensor_index)
    grad_w_output = across_rows(context, middle_rows)
    grad_context = (
        across_cols(middle_rows, output_whole)
        .astype(jnp.bfloat16)
        .reshape(row_count, heads_here, HEAD_DIM)
    )

    def backward_block(totals, block_index):
        grad_key_sum, grad_value_sum = totals
        masked, query_block = block_scores(block_index)
        weights_float = jnp.exp(masked - log_totals[block_index])
        weights_low = weights_float.astype(jnp.bfloat16)
        grad_weights = jnp.einsum(
            "qhd,khd->hqk", grad_context, value_heads, preferred_element_type=jnp.float32
        )
        row_delta = jnp.sum(grad_weights * weights_float, axis=-1, keepdims=True)
        grad_scores = (weights_float * (grad_weights - row_delta)).astype(jnp.bfloat16)
        grad_query_block = (
            jnp.einsum("hqk,khd->qhd", grad_scores, key_heads, preferred_element_type=jnp.float32)
            * scale_factor
        )
        grad_key_sum = (
            grad_key_sum
            + jnp.einsum(
                "hqk,qhd->khd", grad_scores, query_block, preferred_element_type=jnp.float32
            )
            * scale_factor
        )
        grad_value_sum = grad_value_sum + jnp.einsum(
            "hqk,qhd->khd", weights_low, grad_context, preferred_element_type=jnp.float32
        )
        return ((grad_key_sum, grad_value_sum), grad_query_block)

    zero_heads = jnp.zeros((tok_group, heads_here, HEAD_DIM), jnp.float32)
    (grad_key_sum, grad_value_sum), grad_query_blocks = lax.scan(
        backward_block, (zero_heads, zero_heads), jnp.arange(block_count)
    )
    grad_key_flat = grad_key_sum.reshape(tok_group, heads_here * HEAD_DIM)
    grad_value_flat = grad_value_sum.reshape(tok_group, heads_here * HEAD_DIM)
    grad_key_flat = sum_bits(grad_key_flat, low_bits, tensor_index, 0)
    grad_value_flat = sum_bits(grad_value_flat, low_bits, tensor_index, 0)
    grad_queries = grad_query_blocks.reshape(row_count, heads_here * HEAD_DIM).astype(jnp.bfloat16)
    grad_keys = grad_key_flat.astype(jnp.bfloat16)
    grad_values = grad_value_flat.astype(jnp.bfloat16)
    grad_w_query = across_rows(query_rows, grad_queries)
    grad_w_key = across_rows(key_rows, grad_keys)
    grad_w_value = across_rows(value_rows, grad_values)
    grad_w_query = sum_bits(grad_w_query, low_bits, tensor_index, 1)
    grad_w_key = sum_bits(grad_w_key, low_bits, tensor_index, 1)
    grad_w_value = sum_bits(grad_w_value, low_bits, tensor_index, 1)
    grad_w_output = sum_bits(grad_w_output, low_bits, tensor_index, 0)
    stream_partial = jnp.concatenate(
        [
            across_cols(grad_queries, query_whole),
            across_cols(grad_keys, key_whole),
            across_cols(grad_values, value_whole),
        ],
        axis=1,
    )
    grad_streams = sum_bits(stream_partial, high_bits, tensor_index, 0)
    front_grads = front_back(
        (
            grad_streams[:, :model_width],
            grad_streams[:, model_width : 2 * model_width],
            grad_streams[:, 2 * model_width :],
            grad_middle,
        )
    )
    grad_history = front_grads[0].astype(jnp.bfloat16)
    small_sums = lax.psum(
        (
            front_grads[1],
            front_grads[2],
            front_grads[3],
            front_grads[4],
            front_grads[5],
            front_grads[6],
            front_grads[7],
            grad_gain_mlp,
        ),
        ("dp", "tensor"),
    )
    sum_query, sum_key, sum_value, sum_output, sum_expand, sum_reduce = (
        lax.psum_scatter(
            grad_w_query.astype(jnp.bfloat16), "dp", scatter_dimension=0, tiled=True
        ).astype(jnp.float32),
        lax.psum_scatter(
            grad_w_key.astype(jnp.bfloat16), "dp", scatter_dimension=0, tiled=True
        ).astype(jnp.float32),
        lax.psum_scatter(
            grad_w_value.astype(jnp.bfloat16), "dp", scatter_dimension=0, tiled=True
        ).astype(jnp.float32),
        lax.psum_scatter(
            grad_w_output.astype(jnp.bfloat16), "dp", scatter_dimension=1, tiled=True
        ).astype(jnp.float32),
        lax.psum_scatter(
            grad_w_expand.astype(jnp.bfloat16), "dp", scatter_dimension=0, tiled=True
        ).astype(jnp.float32),
        lax.psum_scatter(
            grad_w_reduce.astype(jnp.bfloat16), "dp", scatter_dimension=1, tiled=True
        ).astype(jnp.float32),
    )
    return (
        output,
        grad_history,
        small_sums[0],
        small_sums[1],
        small_sums[2],
        small_sums[3],
        small_sums[4],
        small_sums[5],
        small_sums[6],
        small_sums[7],
        sum_query,
        sum_key,
        sum_value,
        sum_output,
        sum_expand,
        sum_reduce,
    )


def solution(mesh):
    placed = (
        P(None, ("dp", "tensor"), None),
        P(("dp", "tensor"), None),
        P(),
        P(),
        P(),
        P(),
        P(),
        P(),
        P(),
        P(),
        P(),
        P(None, "tensor"),
        P(None, "tensor"),
        P(None, "tensor"),
        P("tensor", None),
        P(None, "tensor"),
        P("tensor", None),
    )
    return jax.shard_map(
        on_device,
        mesh=mesh,
        in_specs=placed,
        out_specs=(
            P(("dp", "tensor"), None),
            P(None, ("dp", "tensor"), None),
            P(),
            P(),
            P(),
            P(),
            P(),
            P(),
            P(),
            P(),
            P("dp", "tensor"),
            P("dp", "tensor"),
            P("dp", "tensor"),
            P("tensor", "dp"),
            P("dp", "tensor"),
            P("tensor", "dp"),
        ),
        check_vma=False,
    )
```

profile of v0, /device:TPU:1, one launch (start us, length us, event | category | flops | bytes accessed | tf_op | source)
XLA Modules:
  0.0 1349.2 jit_solution(5649538605081657744)
XLA Ops:
  16.1 19.8 %fusion.22 = f32[4,128,2048]{2,0,1:T(4,128)S(1)} fusion(f32[128,4,17]{2,1,0:T(4,128)S(1)} %copy.62, bf16[17,128,2048]{2,1,0:T(8,128)(2,1)} %param.17), kind=kOutput, calls=%fused_computation.55 | convolution fusion | flops 213909504 | bytes 13142016 | tf_op jit(solution)/shard_map/jvp(tkj,jtd->ktd)/dot_general | solution.py:35
  51.3 16.1 %collective-permute-done.10 = bf16[128,2048]{1,0:T(8,128)(2,1)} collective-permute-done((bf16[128,2048]{1,0:T(8,128)(2,1)S(1)}, bf16[128,2048]{1,0:T(8,128)(2,1)}, u32[]{:S(2)}, u32[]{:S(2)}) %collective-permute-start.10) | collective-permute-done | bytes 524320 | tf_op jit(solution)/shard_map/ppermute | solution.py:15
  81.2 19.9 %collective-permute-done.6 = bf16[128,2048]{1,0:T(8,128)(2,1)S(1)} collective-permute-done((bf16[128,2048]{1,0:T(8,128)(2,1)S(1)}, bf16[128,2048]{1,0:T(8,128)(2,1)S(1)}, u32[]{:S(2)}, u32[]{:S(2)}) %collective-permute-start.6) | collective-permute-done | bytes 524320 | tf_op jit(solution)/shard_map/ppermute | solution.py:15
  110.7 13.2 collective-permute-done.3
  132.9 13.5 collective-permute-done.9
  151.4 17.4 %collective-permute-done.15 = bf16[1024,512]{0,1:T(8,128)(2,1)S(1)} collective-permute-done((bf16[1024,512]{0,1:T(8,128)(2,1)S(1)}, bf16[1024,512]{0,1:T(8,128)(2,1)S(1)}, u32[]{:S(2)}, u32[]{:S(2)}) %collective-permute-start.15) | collective-permute-done | bytes 1048608 | tf_op jit(solution)/shard_map/ppermute | solution.py:15
  185.5 28.3 %collective-permute-done.5 = bf16[1024,512]{0,1:T(8,128)(2,1)} collective-permute-done((bf16[1024,512]{0,1:T(8,128)(2,1)}, bf16[1024,512]{0,1:T(8,128)(2,1)}, u32[]{:S(2)}, u32[]{:S(2)}) %collective-permute-start.5) | collective-permute-done | bytes 1048608 | tf_op jit(solution)/shard_map/ppermute | solution.py:15
  233.7 16.4 %collective-permute-done.18 = bf16[256,2048]{1,0:T(8,128)(2,1)S(1)} collective-permute-done((bf16[256,2048]{1,0:T(8,128)(2,1)S(1)}, bf16[256,2048]{1,0:T(8,128)(2,1)S(1)}, u32[]{:S(2)}, u32[]{:S(2)}) %collective-permute-start.18) | collective-permute-done | bytes 1048608 | tf_op jit(solution)/shard_map/ppermute | solution.py:15
  254.3 80.8 %collective-permute-done.19 = bf16[128,2048]{1,0:T(8,128)(2,1)S(1)} collective-permute-done((bf16[128,2048]{1,0:T(8,128)(2,1)S(1)}, bf16[128,2048]{1,0:T(8,128)(2,1)S(1)}, u32[]{:S(2)}, u32[]{:S(2)}) %collective-permute-start.19) | collective-permute-done | bytes 524320 | tf_op jit(solution)/shard_map/ppermute | solution.py:15
  338.4 11.0 collective-permute-done.20
  371.8 26.3 %multiply_convert_fusion.1 = (bf16[512,2048]{1,0:T(8,128)(2,1)}, f32[512,2048]{1,0:T(8,128)}, f32[512,2048]{1,0:T(8,128)}) fusion(bf16[2048,1024]{1,0:T(8,128)(2,1)} %copy-done.24, bf16[2048,1024]{1,0:T(8,128)(2,1)} %copy-done.80, pred[]{:T(512)S(6)} %eq.154, bf16[256,2048]{1,0:T(8,128)(2,1)} %copy-done.44, bf16[256,2048]{1,0:T(8,128)(2,1)} %collective-permute-done.21, ...), kind=kOutput, calls=%fused_computation.37 | convolution fusion | flops 4410310656 | bytes 20971522 | tf_op jit(solution)/shard_map/dot_general | solution.py:218
  398.1 52.9 %collective-permute-done.25 = bf16[1024,2048]{1,0:T(8,128)(2,1)} collective-permute-done((bf16[1024,2048]{1,0:T(8,128)(2,1)}, bf16[1024,2048]{1,0:T(8,128)(2,1)}, u32[]{:S(2)}, u32[]{:S(2)}) %collective-permute-start.25) | collective-permute-done | bytes 4194336 | tf_op jit(solution)/shard_map/ppermute | solution.py:15
  451.0 20.3 %add_convert_fusion.2 = bf16[512,2048]{1,0:T(8,128)(2,1)} fusion(f32[512,2048]{1,0:T(8,128)} %get-tuple-element.156, f32[512,2048]{1,0:T(8,128)} %get-tuple-element.171, bf16[1024,2048]{1,0:T(8,128)(2,1)} %maximum_select_fusion.3, bf16[1024,2048]{1,0:T(8,128)(2,1)} %collective-permute-done.25, pred[]{:T(512)S(6)} %eq.154, ...), kind=kOutput, calls=%fused_computation.36 | convolution fusion | flops 4356833280 | bytes 20971522 | tf_op jit(solution)/shard_map/dot_general | solution.py:55
  471.3 10.6 fusion.27
  501.3 34.4 %collective-permute-done.30 = bf16[256,2048]{1,0:T(8,128)(2,1)} collective-permute-done((bf16[256,2048]{1,0:T(8,128)(2,1)S(1)}, bf16[256,2048]{1,0:T(8,128)(2,1)}, u32[]{:S(2)}, u32[]{:S(2)}) %collective-permute-start.30) | collective-permute-done | bytes 1048608 | tf_op jit(solution)/shard_map/ppermute | solution.py:15
  598.7 14.3 %multiply_reduce_fusion = (f32[4,512]{1,0:T(4,128)S(1)}, f32[4,512,2048]{2,1,0:T(8,128)}) fusion(f32[4,512,2048]{2,1,0:T(8,128)} %get-tuple-element.170, f32[4,512]{1,0:T(4,128)S(1)} %log_add_fusion, bf16[512,4,128]{0,2,1:T(8,128)(2,1)S(1)} %bitcast.140, bf16[1024,4,128]{0,2,1:T(8,128)(2,1)S(1)} %copy-done.29, bf16[1024,4,128]{0,2,1:T(8,128)(2,1)} %bitcast.5, ...), kind=kOutput, calls=%fused_computation.3 | convolution fusion | flops 1095759872 | bytes 36192256 | tf_op jit(solution)/shard_map/while/body/eval_jaxpr/qhd,khd->hqk/dot_general | solution.py:252
  613.1 15.9 %multiply_convert_fusion = bf16[4,512,2048]{2,1,0:T(8,128)(2,1)} fusion(f32[4,512,2048]{2,1,0:T(8,128)} %get-tuple-element.173, f32[4,512,2048]{2,1,0:T(8,128)} %get-tuple-element.170, f32[4,512]{1,0:T(4,128)S(1)} %get-tuple-element.172, f32[4,512]{1,0:T(4,128)S(1)} %log_add_fusion), kind=kLoop, calls=%fused_computation.2 | loop fusion | flops 16777216 | bytes 41959424 | tf_op jit(solution)/shard_map/while/body/eval_jaxpr/convert_element_type | solution.py:256
  651.4 121.1 %collective-permute-done.46 = bf16[256,2048]{1,0:T(8,128)(2,1)S(1)} collective-permute-done((bf16[256,2048]{1,0:T(8,128)(2,1)S(1)}, bf16[256,2048]{1,0:T(8,128)(2,1)S(1)}, u32[]{:S(2)}, u32[]{:S(2)}) %collective-permute-start.46) | collective-permute-done | bytes 1048608 | tf_op jit(solution)/shard_map/ppermute | solution.py:15
  774.2 20.8 %collective-permute-done.36 = bf16[1024,512]{0,1:T(8,128)(2,1)S(1)} collective-permute-done((bf16[1024,512]{0,1:T(8,128)(2,1)S(1)}, bf16[1024,512]{0,1:T(8,128)(2,1)S(1)}, u32[]{:S(2)}, u32[]{:S(2)}) %collective-permute-start.36) | collective-permute-done | bytes 1048608 | tf_op jit(solution)/shard_map/ppermute | solution.py:15
  795.0 12.9 collective-permute-start.47
  817.5 12.9 collective-permute-start.37
  897.2 16.3 %collective-permute-done.42 = bf16[2048,256]{1,0:T(8,128)(2,1)} collective-permute-done((bf16[2048,256]{1,0:T(8,128)(2,1)}, bf16[2048,256]{1,0:T(8,128)(2,1)}, u32[]{:S(2)}, u32[]{:S(2)}) %collective-permute-start.42) | collective-permute-done | bytes 1048608 | tf_op jit(solution)/shard_map/ppermute | solution.py:15
  917.7 11.7 convert_add_fusion
  943.4 18.8 %collective-permute-done.38 = bf16[256,6144]{1,0:T(8,128)(2,1)} collective-permute-done((bf16[256,6144]{1,0:T(8,128)(2,1)}, bf16[256,6144]{1,0:T(8,128)(2,1)}, u32[]{:S(2)}, u32[]{:S(2)}) %collective-permute-start.38) | collective-permute-done | bytes 3145760 | tf_op jit(solution)/shard_map/ppermute | solution.py:15
  976.9 29.3 %reduce-scatter.7.cloned.1.call-done = bf16[256,128]{1,0:T(8,128)(2,1)} async-done(((bf16[2048,128]{1,0:T(8,128)(2,1)}), bf16[256,128]{1,0:T(8,128)(2,1)}) %reduce-scatter.7.cloned.1.call-update) | async-done | bytes 65552 | tf_op jit(solution)/shard_map/reduce_scatter | solution.py:323
  1014.0 65.8 %reduce-scatter.11.cloned.1.call-done = bf16[256,128]{1,0:T(8,128)(2,1)} async-done(((bf16[2048,128]{1,0:T(8,128)(2,1)}), bf16[256,128]{1,0:T(8,128)(2,1)}) %reduce-scatter.11.cloned.1.call-update) | async-done | bytes 65552 | tf_op jit(solution)/shard_map/reduce_scatter | solution.py:329
  1081.3 71.9 %reduce-scatter.9.cloned.1.call-done = bf16[256,128]{1,0:T(8,128)(2,1)} async-done(((bf16[2048,128]{1,0:T(8,128)(2,1)}), bf16[256,128]{1,0:T(8,128)(2,1)}) %reduce-scatter.9.cloned.1.call-update) | async-done | bytes 65552 | tf_op jit(solution)/shard_map/reduce_scatter | solution.py:326
  1164.7 17.9 %fusion.113 = (f32[4,17]{1,0:T(4,128)S(1)}, f32[128,4,17]{2,1,0:T(4,128)S(1)}) fusion(bf16[17,128,2048]{2,1,0:T(8,128)(2,1)S(1)} %bitcast.136, f32[128,2048,4]{1,0,2:T(8,128)S(1)} %add_bitcast_fusion), kind=kOutput, calls=%fused_computation.270 | convolution fusion | flops 213918144 | bytes 13142288 | tf_op jit(solution)/shard_map/transpose(jvp(tkj,jtd->ktd))/dot_general | solution.py:35
  1190.6 25.6 %fusion = bf16[17,128,2048]{2,0,1:T(8,128)(2,1)} fusion(f32[1,128,2048]{2,0,1:T(1,128)S(1)} %broadcast_in_dim.111, f32[128,4,17]{2,1,0:T(4,128)S(1)} %copy-done.33, f32[128,2048,4]{1,0,2:T(8,128)} %copy-done.25), kind=kOutput, calls=%fused_computation.1 | convolution fusion | flops 222822400 | bytes 14190592 | tf_op jit(solution)/shard_map/transpose(jvp(tkj,jtd->ktd))/dot_general | solution.py:35
  1216.2 13.6 %copy.76 = bf16[17,128,2048]{2,1,0:T(8,128)(2,1)} copy(bf16[17,128,2048]{2,0,1:T(8,128)(2,1)} %fusion) | data formatting | bytes 17825792
  1230.1 69.4 %all-reduce.5 = (f32[2048]{0:T(1024)}, f32[68,68]{1,0:T(8,128)}, f32[68]{0:T(128)}, f32[2048]{0:T(1024)}, f32[2048]{0:T(1024)}, /*index=5*/f32[2048]{0:T(1024)}, f32[2048]{0:T(1024)}) all-reduce(f32[2048]{0:T(1024)S(1)} %get-tuple-element.133, f32[68,68]{1,0:T(8,128)S(1)} %fusion.72, ...), channel_id=1, replica_groups=mesh['dp'=8,'tensor'=16] {'dp','tensor'}, use_global_device_ids=true, to_apply=%region_17.18 | all-reduce | flops 14932 | bytes 119456 | tf_op jit(solution)/shard_map/psum | solution.py:309
  1312.0 27.4 %all-reduce.8.cloned.1.call-done = f32[2048,68]{0,1:T(8,128)} async-done(((f32[2048,68]{0,1:T(8,128)}), f32[2048,68]{0,1:T(8,128)}) %all-reduce.8.cloned.1.call-update) | async-done | bytes 557072 | tf_op jit(solution)/shard_map/psum | solution.py:309
  (456 shorter events, 384.7 us)
Async XLA Ops:
  8.0 967.4 %reduce-scatter.13.cloned.1.call-start = ((), (), s32[]{:S(2)}) async-start(), calls=%async_computation.10 | async-start | bytes 589824 | tf_op jit(solution)/shard_map/reduce_scatter | solution.py:332
  8.1 68.1 %collective-permute-start.8 = (bf16[2048,128]{1,0:T(8,128)(2,1)}, bf16[2048,128]{1,0:T(8,128)(2,1)}, u32[]{:S(2)}, u32[]{:S(2)}) collective-permute-start(bf16[2048,128]{1,0:T(8,128)(2,1)} %param.28), channel_id=1, source_target_pairs={{0,1},{1,0},{2,3},{3,2},{4,5},{5,4},{6,7},{7,6},{8,9},{9,8},{10,11... | collective-permute-start | bytes 1572872 | tf_op jit(solution)/shard_map/ppermute | solution.py:15
  9.7 61.6 %collective-permute-start.2 = (bf16[2048,128]{1,0:T(8,128)(2,1)}, bf16[2048,128]{1,0:T(8,128)(2,1)}, u32[]{:S(2)}, u32[]{:S(2)}) collective-permute-start(bf16[2048,128]{1,0:T(8,128)(2,1)} %param.30), channel_id=1, source_target_pairs={{0,1},{1,0},{2,3},{3,2},{4,5},{5,4},{6,7},{7,6},{8,9},{9,8},{10,11... | collective-permute-start | bytes 1572872 | tf_op jit(solution)/shard_map/ppermute | solution.py:15
  50.0 52.6 %collective-permute-start.13 = (bf16[2048,256]{1,0:T(8,128)(2,1)}, bf16[2048,256]{1,0:T(8,128)(2,1)}, u32[]{:S(2)}, u32[]{:S(2)}) collective-permute-start(bf16[2048,256]{1,0:T(8,128)(2,1)} %maximum_select_fusion.29), channel_id=1, source_target_pairs={{0,2},{1,3},{2,0},{3,1},{4,6},{5,7},{6,4},{7,5},{8,10},{9,11},{10,... | collective-permute-start | bytes 3145736 | tf_op jit(solution)/shard_map/ppermute | solution.py:15
  76.1 47.7 %collective-permute-start.3 = (bf16[2048,256]{1,0:T(8,128)(2,1)S(1)}, bf16[2048,256]{1,0:T(8,128)(2,1)S(1)}, u32[]{:S(2)}, u32[]{:S(2)}) collective-permute-start(bf16[2048,256]{1,0:T(8,128)(2,1)S(1)} %maximum_select_fusion.23), channel_id=1, source_target_pairs={{0,2},{1,3},{2,0},{3,1},{4,6},{5,7},{6,4},{7,5},{8,10},{9,11},{10,... | collective-permute-start | bytes 3145736 | tf_op jit(solution)/shard_map/ppermute | solution.py:15
  78.5 67.9 %collective-permute-start.9 = (bf16[2048,256]{1,0:T(8,128)(2,1)S(1)}, bf16[2048,256]{1,0:T(8,128)(2,1)S(1)}, u32[]{:S(2)}, u32[]{:S(2)}) collective-permute-start(bf16[2048,256]{1,0:T(8,128)(2,1)S(1)} %maximum_select_fusion.27), channel_id=1, source_target_pairs={{0,2},{1,3},{2,0},{3,1},{4,6},{5,7},{6,4},{7,5},{8,10},{9,11},{10,... | collective-permute-start | bytes 3145736 | tf_op jit(solution)/shard_map/ppermute | solution.py:15
  102.6 45.0 %collective-permute-start.7 = (bf16[256,2048]{1,0:T(8,128)(2,1)S(1)}, bf16[256,2048]{1,0:T(8,128)(2,1)S(1)}, u32[]{:S(2)}, u32[]{:S(2)}) collective-permute-start(bf16[256,2048]{1,0:T(8,128)(2,1)S(1)} %maximum_select_fusion.26), channel_id=1, source_target_pairs={{0,8},{1,9},{2,10},{3,11},{4,12},{5,13},{6,14},{7,15},{8,0},{9,1},... | collective-permute-start | bytes 3145736 | tf_op jit(solution)/shard_map/ppermute | solution.py:15
  125.2 102.2 %collective-permute-start.22 = (bf16[2048,512]{1,0:T(8,128)(2,1)}, bf16[2048,512]{1,0:T(8,128)(2,1)}, u32[]{:S(2)}, u32[]{:S(2)}) collective-permute-start(bf16[2048,512]{1,0:T(8,128)(2,1)} %param.32), channel_id=1, source_target_pairs={{0,1},{1,0},{2,3},{3,2},{4,5},{5,4},{6,7},{7,6},{8,9},{9,8},{10,11... | collective-permute-start | bytes 6291464 | tf_op jit(solution)/shard_map/ppermute | solution.py:15
  146.4 75.9 %collective-permute-start.17 = (bf16[256,2048]{1,0:T(8,128)(2,1)}, bf16[256,2048]{1,0:T(8,128)(2,1)}, u32[]{:S(2)}, u32[]{:S(2)}) collective-permute-start(bf16[256,2048]{1,0:T(8,128)(2,1)} %maximum_select_fusion.32), channel_id=1, source_target_pairs={{0,2},{1,3},{2,0},{3,1},{4,6},{5,7},{6,4},{7,5},{8,10},{9,11},{10,... | collective-permute-start | bytes 3145736 | tf_op jit(solution)/shard_map/ppermute | solution.py:15
  150.2 63.7 %collective-permute-start.5 = (bf16[1024,512]{0,1:T(8,128)(2,1)}, bf16[1024,512]{0,1:T(8,128)(2,1)}, u32[]{:S(2)}, u32[]{:S(2)}) collective-permute-start(bf16[1024,512]{0,1:T(8,128)(2,1)} %maximum_select_fusion.24), channel_id=1, source_target_pairs={{0,2},{1,3},{2,0},{3,1},{4,6},{5,7},{6,4},{7,5},{8,10},{9,11},{10,... | collective-permute-start | bytes 3145736 | tf_op jit(solution)/shard_map/ppermute | solution.py:15
  232.5 131.4 %collective-permute-start.23 = (bf16[2048,1024]{1,0:T(8,128)(2,1)S(1)}, bf16[2048,1024]{1,0:T(8,128)(2,1)S(1)}, u32[]{:S(2)}, u32[]{:S(2)}) collective-permute-start(bf16[2048,1024]{1,0:T(8,128)(2,1)S(1)} %maximum_select_fusion.2), channel_id=1, source_target_pairs={{0,2},{1,3},{2,0},{3,1},{4,6},{5,7},{6,4},{7,5},{8,10},{9,11},{10,... | collective-permute-start | bytes 12582920 | tf_op jit(solution)/shard_map/ppermute | solution.py:15
  250.6 84.5 %collective-permute-start.19 = (bf16[128,2048]{1,0:T(8,128)(2,1)S(1)}, bf16[128,2048]{1,0:T(8,128)(2,1)S(1)}, u32[]{:S(2)}, u32[]{:S(2)}) collective-permute-start(bf16[128,2048]{1,0:T(8,128)(2,1)S(1)} %select_convert_fusion.23), channel_id=1, source_target_pairs={{0,4},{1,5},{2,6},{3,7},{4,0},{5,1},{6,2},{7,3},{8,12},{9,13},{10,... | collective-permute-start | bytes 1572872 | tf_op jit(solution)/shard_map/ppermute | solution.py:15
  252.2 99.6 %collective-permute-start.24 = (bf16[512,2048]{1,0:T(8,128)(2,1)S(1)}, bf16[512,2048]{1,0:T(8,128)(2,1)S(1)}, u32[]{:S(2)}, u32[]{:S(2)}) collective-permute-start(bf16[512,2048]{1,0:T(8,128)(2,1)S(1)} %copy-done.31), channel_id=1, source_target_pairs={{0,1},{1,0},{2,3},{3,2},{4,5},{5,4},{6,7},{7,6},{8,9},{9,8},{10,11... | collective-permute-start | bytes 6291464 | tf_op jit(solution)/shard_map/ppermute | solution.py:15
  355.6 95.4 %collective-permute-start.25 = (bf16[1024,2048]{1,0:T(8,128)(2,1)}, bf16[1024,2048]{1,0:T(8,128)(2,1)}, u32[]{:S(2)}, u32[]{:S(2)}) collective-permute-start(bf16[1024,2048]{1,0:T(8,128)(2,1)} %maximum_select_fusion.3), channel_id=1, source_target_pairs={{0,2},{1,3},{2,0},{3,1},{4,6},{5,7},{6,4},{7,5},{8,10},{9,11},{10,... | collective-permute-start | bytes 12582920 | tf_op jit(solution)/shard_map/ppermute | solution.py:15
  492.6 47.8 %collective-permute-start.26 = (bf16[256,2048]{1,0:T(8,128)(2,1)S(1)}, bf16[256,2048]{1,0:T(8,128)(2,1)}, u32[]{:S(2)}, u32[]{:S(2)}) collective-permute-start(bf16[256,2048]{1,0:T(8,128)(2,1)S(1)} %select_convert_fusion.13), channel_id=1, source_target_pairs={{0,8},{1,9},{2,10},{3,11},{4,12},{5,13},{6,14},{7,15},{8,0},{9,1},... | collective-permute-start | bytes 3145736 | tf_op jit(solution)/shard_map/ppermute | solution.py:15
  565.6 281.5 %collective-permute-start.48 = (bf16[2048,1024]{1,0:T(8,128)(2,1)}, bf16[2048,1024]{1,0:T(8,128)(2,1)}, u32[]{:S(2)}, u32[]{:S(2)}) collective-permute-start(bf16[2048,1024]{1,0:T(8,128)(2,1)} %select_convert_fusion.1), channel_id=1, source_target_pairs={{0,2},{1,3},{2,0},{3,1},{4,6},{5,7},{6,4},{7,5},{8,10},{9,11},{10,... | collective-permute-start | bytes 12582920 | tf_op jit(solution)/shard_map/ppermute | solution.py:15
  588.3 329.4 %collective-permute-start.50 = (bf16[1024,2048]{1,0:T(8,128)(2,1)}, bf16[1024,2048]{1,0:T(8,128)(2,1)}, u32[]{:S(2)}, u32[]{:S(2)}) collective-permute-start(bf16[1024,2048]{1,0:T(8,128)(2,1)} %select_convert_fusion), channel_id=1, source_target_pairs={{0,2},{1,3},{2,0},{3,1},{4,6},{5,7},{6,4},{7,5},{8,10},{9,11},{10,... | collective-permute-start | bytes 12582920 | tf_op jit(solution)/shard_map/ppermute | solution.py:15
  642.1 130.5 %collective-permute-start.46 = (bf16[256,2048]{1,0:T(8,128)(2,1)S(1)}, bf16[256,2048]{1,0:T(8,128)(2,1)S(1)}, u32[]{:S(2)}, u32[]{:S(2)}) collective-permute-start(bf16[256,2048]{1,0:T(8,128)(2,1)S(1)} %select_convert_fusion.6), channel_id=1, source_target_pairs={{0,2},{1,3},{2,0},{3,1},{4,6},{5,7},{6,4},{7,5},{8,10},{9,11},{10,... | collective-permute-start | bytes 3145736 | tf_op jit(solution)/shard_map/ppermute | solution.py:15
  643.4 151.7 %collective-permute-start.36 = (bf16[1024,512]{0,1:T(8,128)(2,1)S(1)}, bf16[1024,512]{0,1:T(8,128)(2,1)S(1)}, u32[]{:S(2)}, u32[]{:S(2)}) collective-permute-start(bf16[1024,512]{0,1:T(8,128)(2,1)S(1)} %bitcast.146), channel_id=1, source_target_pairs={{0,2},{1,3},{2,0},{3,1},{4,6},{5,7},{6,4},{7,5},{8,10},{9,11},{10,... | collective-permute-start | bytes 3145736 | tf_op jit(solution)/shard_map/ppermute | solution.py:15
  644.1 173.4 %collective-permute-start.34 = (bf16[1024,512]{0,1:T(8,128)(2,1)S(1)}, bf16[1024,512]{0,1:T(8,128)(2,1)S(1)}, u32[]{:S(2)}, u32[]{:S(2)}) collective-permute-start(bf16[1024,512]{0,1:T(8,128)(2,1)S(1)} %bitcast.145), channel_id=1, source_target_pairs={{0,2},{1,3},{2,0},{3,1},{4,6},{5,7},{6,4},{7,5},{8,10},{9,11},{10,... | collective-permute-start | bytes 3145736 | tf_op jit(solution)/shard_map/ppermute | solution.py:15
  772.6 67.4 %collective-permute-start.40 = (bf16[2048,256]{1,0:T(8,128)(2,1)S(1)}, bf16[2048,256]{1,0:T(8,128)(2,1)S(1)}, u32[]{:S(2)}, u32[]{:S(2)}) collective-permute-start(bf16[2048,256]{1,0:T(8,128)(2,1)S(1)} %select_convert_fusion.9), channel_id=1, source_target_pairs={{0,2},{1,3},{2,0},{3,1},{4,6},{5,7},{6,4},{7,5},{8,10},{9,11},{10,... | collective-permute-start | bytes 3145736 | tf_op jit(solution)/shard_map/ppermute | solution.py:15
  795.0 63.3 %collective-permute-start.47 = (bf16[128,2048]{1,0:T(8,128)(2,1)}, bf16[128,2048]{1,0:T(8,128)(2,1)}, u32[]{:S(2)}, u32[]{:S(2)}) collective-permute-start(bf16[128,2048]{1,0:T(8,128)(2,1)} %select_convert_fusion.15), channel_id=1, source_target_pairs={{0,1},{1,0},{2,3},{3,2},{4,5},{5,4},{6,7},{7,6},{8,9},{9,8},{10,11... | collective-permute-start | bytes 1572872 | tf_op jit(solution)/shard_map/ppermute | solution.py:15
  858.3 78.3 %collective-permute-start.49 = (bf16[2048,512]{1,0:T(8,128)(2,1)}, bf16[2048,512]{1,0:T(8,128)(2,1)}, u32[]{:S(2)}, u32[]{:S(2)}) collective-permute-start(bf16[2048,512]{1,0:T(8,128)(2,1)} %select_convert_fusion.4), channel_id=1, source_target_pairs={{0,1},{1,0},{2,3},{3,2},{4,5},{5,4},{6,7},{7,6},{8,9},{9,8},{10,11... | collective-permute-start | bytes 6291464 | tf_op jit(solution)/shard_map/ppermute | solution.py:15
  860.9 145.3 %reduce-scatter.7.cloned.1.call-start = ((), (), s32[]{:S(2)}) async-start(), calls=%async_computation.7 | async-start | bytes 589824 | tf_op jit(solution)/shard_map/reduce_scatter | solution.py:323
  889.5 72.7 %collective-permute-start.38 = (bf16[256,6144]{1,0:T(8,128)(2,1)}, bf16[256,6144]{1,0:T(8,128)(2,1)}, u32[]{:S(2)}, u32[]{:S(2)}) collective-permute-start(bf16[256,6144]{1,0:T(8,128)(2,1)} %select_convert_fusion.2), channel_id=1, source_target_pairs={{0,8},{1,9},{2,10},{3,11},{4,12},{5,13},{6,14},{7,15},{8,0},{9,1},... | collective-permute-start | bytes 9437192 | tf_op jit(solution)/shard_map/ppermute | solution.py:15
  892.9 186.9 %reduce-scatter.11.cloned.1.call-start = ((), (), s32[]{:S(2)}) async-start(), calls=%async_computation.9 | async-start | bytes 589824 | tf_op jit(solution)/shard_map/reduce_scatter | solution.py:329
  917.7 235.6 %reduce-scatter.9.cloned.1.call-start = ((), (), s32[]{:S(2)}) async-start(), calls=%async_computation.8 | async-start | bytes 589824 | tf_op jit(solution)/shard_map/reduce_scatter | solution.py:326
  931.4 368.1 %reduce-scatter.15.cloned.1.call-start = ((), (), s32[]{:S(2)}) async-start(), calls=%async_computation.11 | async-start | bytes 2359296 | tf_op jit(solution)/shard_map/reduce_scatter | solution.py:335
  936.6 71.1 %collective-permute-start.51 = (bf16[512,2048]{1,0:T(8,128)(2,1)}, bf16[512,2048]{1,0:T(8,128)(2,1)S(1)}, u32[]{:S(2)}, u32[]{:S(2)}) collective-permute-start(bf16[512,2048]{1,0:T(8,128)(2,1)} %select_convert_fusion.3), channel_id=1, source_target_pairs={{0,1},{1,0},{2,3},{3,2},{4,5},{5,4},{6,7},{7,6},{8,9},{9,8},{10,11... | collective-permute-start | bytes 6291464 | tf_op jit(solution)/shard_map/ppermute | solution.py:15
  943.3 366.9 %reduce-scatter.17.cloned.1.call-start = ((), (), s32[]{:S(2)}) async-start(), calls=%async_computation.12 | async-start | bytes 2359296 | tf_op jit(solution)/shard_map/reduce_scatter | solution.py:338
  973.8 181.0 %collective-permute-start.39 = (bf16[128,6144]{1,0:T(8,128)(2,1)}, bf16[128,6144]{1,0:T(8,128)(2,1)}, u32[]{:S(2)}, u32[]{:S(2)}) collective-permute-start(bf16[128,6144]{1,0:T(8,128)(2,1)} %select_convert_fusion.5), channel_id=1, source_target_pairs={{0,4},{1,5},{2,6},{3,7},{4,0},{5,1},{6,2},{7,3},{8,12},{9,13},{10,... | collective-permute-start | bytes 4718600 | tf_op jit(solution)/shard_map/ppermute | solution.py:15
  1013.8 325.6 %all-reduce.8.cloned.1.call-start = ((), (), s32[]{:S(2)}) async-start(), calls=%async_computation.6 | async-start | bytes 1179648 | tf_op jit(solution)/shard_map/psum | solution.py:309
  (132 other events, 2096.6 us)
Sparse Core Ops, SparseCore 0:
  861.0 71.6 reduce-scatter.12
  936.8 69.4 reduce-scatter.6
  1010.8 68.9 reduce-scatter.10
  1083.8 69.4 reduce-scatter.8
  1157.3 74.6 reduce-scatter.14
  1235.9 74.2 reduce-scatter.16
Sparse Core Ops, SparseCore 1:
  1190.6 148.7 all-reduce.7
where the time goes:
time: 1350 us
  waiting for transfers between devices  731 us (54%)
  matrix products  235 us (17%)
  other arithmetic  157 us (12%)
  starting transfers between devices  90.5 us (7%)
  blocking collectives  69.4 us (5%)
  local copies, waits for them, and re-layouts  49.2 us (4%)
  between operations  17.8 us (1%)
    ppermute x52, waiting for transfers between devices, swapped(): lax.ppermute(x, axis, [(i, i ^ 1 << bit) for i in range(lax.axis_size(axi...  528 us
    ppermute x52, starting transfers between devices, swapped(): lax.ppermute(x, axis, [(i, i ^ 1 << bit) for i in range(lax.axis_size(axi...  90.1 us
    reduce_scatter x1, waiting for transfers between devices, on_device(): lax.psum_scatter(grad_w_key.astype(jnp.bfloat16), 'dp', scatter_dimension...  71.9 us
    psum x1, blocking collectives, on_device(): lax.psum((front_grads[1], front_grads[2], front_grads[3], front_grads[4],...  69.4 us
    reduce_scatter x1, waiting for transfers between devices, on_device(): lax.psum_scatter(grad_w_value.astype(jnp.bfloat16), 'dp', scatter_dimensi...  65.8 us
    dot_general x3, matrix products, front_part(): jnp.einsum('tkj,jtd->ktd', mixing, history_float, precision=PRECISE)  63.3 us
    unnamed x212, local copies, waits for them, and re-layouts  44.7 us
    dot_general x6, matrix products, across_cols(): lax.dot_general(left_side, right_side, (((1,), (1,)), ((), ())), preferre...  43.8 us
  transfers between devices with their start and end apart: 59, of which 27 were waited for; matrix products, arithmetic and copies ran while one was open for 27% of the time, Pallas kernels for 0%

commit v1 on v0

--- a/solution.py
+++ b/solution.py
@@ -307,17 +307,20 @@
     )
     grad_history = front_grads[0].astype(jnp.bfloat16)
     small_sums = lax.psum(
-        (
-            front_grads[1],
-            front_grads[2],
-            front_grads[3],
-            front_grads[4],
-            front_grads[5],
-            front_grads[6],
-            front_grads[7],
-            grad_gain_mlp,
+        lax.psum(
+            (
+                front_grads[1],
+                front_grads[2],
+                front_grads[3],
+                front_grads[4],
+                front_grads[5],
+                front_grads[6],
+                front_grads[7],
+                grad_gain_mlp,
+            ),
+            "dp",
         ),
-        ("dp", "tensor"),
+        "tensor",
     )
     sum_query, sum_key, sum_value, sum_output, sum_expand, sum_reduce = (
         lax.psum_scatter(

time: 1350 us -> 1520 us (1.13)
  waiting for transfers between devices: 731 us -> 884 us
  blocking collectives: 69.4 us -> 95 us
    psum x0 -> x1, waiting for transfers between devices: none -> 116 us  [on_device(): lax.psum(lax.psum((front_grads[1], front_grads[2], front_grads[3], front_...]
    psum x0 -> x1, blocking collectives: none -> 63 us  [on_device(): lax.psum(lax.psum((front_grads[1], front_grads[2], front_grads[3], front_...]
    psum x1, waiting for transfers between devices: 27.4 us -> 78.7 us  [on_device(): lax.psum((front_grads[1], front_grads[2], front_grads[3], front_grads[4],...]
    ppermute x52, waiting for transfers between devices: 528 us -> 578 us  [swapped(): lax.ppermute(x, axis, [(i, i ^ 1 << bit) for i in range(lax.axis_size(axi...]
    reduce_scatter x1, waiting for transfers between devices: 65.8 us -> 16.9 us  [on_device(): lax.psum_scatter(grad_w_value.astype(jnp.bfloat16), 'dp', scatter_dimensi...]
    psum x1, blocking collectives: 69.4 us -> 31.9 us  [on_device(): lax.psum((front_grads[1], front_grads[2], front_grads[3], front_grads[4],...]
    reduce_scatter x1, waiting for transfers between devices: 29.3 us -> 0.01 us  [on_device(): lax.psum_scatter(grad_w_query.astype(jnp.bfloat16), 'dp', scatter_dimensi...]
    unnamed x212 -> x204, local copies, waits for them, and re-layouts: 44.7 us -> 36.7 us
  transfers between devices with their start and end apart: 59 -> 60, of which waited for: 27 -> 30; matrix products, arithmetic and copies ran while one was open for 27% -> 24% of each run, Pallas kernels for 0% -> 0%
where the time goes in v1:
time: 1520 us
  waiting for transfers between devices  884 us (58%)
  matrix products  236 us (16%)
  other arithmetic  151 us (10%)
  blocking collectives  95 us (6%)
  starting transfers between devices  93.3 us (6%)
  local copies, waits for them, and re-layouts  41.1 us (3%)
  between operations  16.2 us (1%)
    ppermute x52, waiting for transfers between devices, swapped(): lax.ppermute(x, axis, [(i, i ^ 1 << bit) for i in range(lax.axis_size(axi...  578 us
    psum x1, waiting for transfers between devices, on_device(): lax.psum(lax.psum((front_grads[1], front_grads[2], front_grads[3], front_...  116 us
    ppermute x52, starting transfers between devices, swapped(): lax.ppermute(x, axis, [(i, i ^ 1 << bit) for i in range(lax.axis_size(axi...  92.6 us
    psum x1, waiting for transfers between devices, on_device(): lax.psum((front_grads[1], front_grads[2], front_grads[3], front_grads[4],...  78.7 us
    reduce_scatter x1, waiting for transfers between devices, on_device(): lax.psum_scatter(grad_w_key.astype(jnp.bfloat16), 'dp', scatter_dimension...  72.3 us
    dot_general x3, matrix products, front_part(): jnp.einsum('tkj,jtd->ktd', mixing, history_float, precision=PRECISE)  63.2 us
    psum x1, blocking collectives, on_device(): lax.psum(lax.psum((front_grads[1], front_grads[2], front_grads[3], front_...  63 us
    dot_general x6, matrix products, across_cols(): lax.dot_general(left_side, right_side, (((1,), (1,)), ((), ())), preferre...  43.8 us
  transfers between devices with their start and end apart: 60, of which 30 were waited for; matrix products, arithmetic and copies ran while one was open for 24% of the time, Pallas kernels for 0%

profile of v1, /device:TPU:1, one launch (start us, length us, event | category | flops | bytes accessed | tf_op | source)
XLA Modules:
  0.0 1517.1 jit_solution(8852213992614347593)
XLA Ops:
  15.3 19.8 %fusion.22 = f32[4,128,2048]{2,0,1:T(4,128)S(1)} fusion(f32[128,4,17]{2,1,0:T(4,128)S(1)} %copy.62, bf16[17,128,2048]{2,1,0:T(8,128)(2,1)} %param.17), kind=kOutput, calls=%fused_computation.55 | convolution fusion | flops 213909504 | bytes 13142016 | tf_op jit(solution)/shard_map/jvp(tkj,jtd->ktd)/dot_general | solution.py:35
  50.3 16.2 %collective-permute-done.10 = bf16[128,2048]{1,0:T(8,128)(2,1)} collective-permute-done((bf16[128,2048]{1,0:T(8,128)(2,1)S(1)}, bf16[128,2048]{1,0:T(8,128)(2,1)}, u32[]{:S(2)}, u32[]{:S(2)}) %collective-permute-start.10) | collective-permute-done | bytes 524320 | tf_op jit(solution)/shard_map/ppermute | solution.py:15
  80.4 19.8 %collective-permute-done.6 = bf16[128,2048]{1,0:T(8,128)(2,1)S(1)} collective-permute-done((bf16[128,2048]{1,0:T(8,128)(2,1)S(1)}, bf16[128,2048]{1,0:T(8,128)(2,1)S(1)}, u32[]{:S(2)}, u32[]{:S(2)}) %collective-permute-start.6) | collective-permute-done | bytes 524320 | tf_op jit(solution)/shard_map/ppermute | solution.py:15
  109.8 13.2 collective-permute-done.3
  132.0 13.5 collective-permute-done.9
  150.5 17.4 %collective-permute-done.15 = bf16[1024,512]{0,1:T(8,128)(2,1)S(1)} collective-permute-done((bf16[1024,512]{0,1:T(8,128)(2,1)S(1)}, bf16[1024,512]{0,1:T(8,128)(2,1)S(1)}, u32[]{:S(2)}, u32[]{:S(2)}) %collective-permute-start.15) | collective-permute-done | bytes 1048608 | tf_op jit(solution)/shard_map/ppermute | solution.py:15
  184.7 28.3 %collective-permute-done.5 = bf16[1024,512]{0,1:T(8,128)(2,1)} collective-permute-done((bf16[1024,512]{0,1:T(8,128)(2,1)}, bf16[1024,512]{0,1:T(8,128)(2,1)}, u32[]{:S(2)}, u32[]{:S(2)}) %collective-permute-start.5) | collective-permute-done | bytes 1048608 | tf_op jit(solution)/shard_map/ppermute | solution.py:15
  232.8 16.3 %collective-permute-done.18 = bf16[256,2048]{1,0:T(8,128)(2,1)S(1)} collective-permute-done((bf16[256,2048]{1,0:T(8,128)(2,1)S(1)}, bf16[256,2048]{1,0:T(8,128)(2,1)S(1)}, u32[]{:S(2)}, u32[]{:S(2)}) %collective-permute-start.18) | collective-permute-done | bytes 1048608 | tf_op jit(solution)/shard_map/ppermute | solution.py:15
  253.4 80.9 %collective-permute-done.19 = bf16[128,2048]{1,0:T(8,128)(2,1)S(1)} collective-permute-done((bf16[128,2048]{1,0:T(8,128)(2,1)S(1)}, bf16[128,2048]{1,0:T(8,128)(2,1)S(1)}, u32[]{:S(2)}, u32[]{:S(2)}) %collective-permute-start.19) | collective-permute-done | bytes 524320 | tf_op jit(solution)/shard_map/ppermute | solution.py:15
  371.0 26.4 %multiply_convert_fusion.1 = (bf16[512,2048]{1,0:T(8,128)(2,1)}, f32[512,2048]{1,0:T(8,128)}, f32[512,2048]{1,0:T(8,128)}) fusion(bf16[2048,1024]{1,0:T(8,128)(2,1)} %copy-done.19, bf16[2048,1024]{1,0:T(8,128)(2,1)} %copy-done.76, pred[]{:T(512)S(6)} %eq.154, bf16[256,2048]{1,0:T(8,128)(2,1)} %copy-done.38, bf16[256,2048]{1,0:T(8,128)(2,1)} %collective-permute-done.21, ...), kind=kOutput, calls=%fused_computation.37 | convolution fusion | flops 4410310656 | bytes 20971522 | tf_op jit(solution)/shard_map/dot_general | solution.py:218
  397.5 52.7 %collective-permute-done.25 = bf16[1024,2048]{1,0:T(8,128)(2,1)} collective-permute-done((bf16[1024,2048]{1,0:T(8,128)(2,1)}, bf16[1024,2048]{1,0:T(8,128)(2,1)}, u32[]{:S(2)}, u32[]{:S(2)}) %collective-permute-start.25) | collective-permute-done | bytes 4194336 | tf_op jit(solution)/shard_map/ppermute | solution.py:15
  450.1 20.4 %add_convert_fusion.2 = bf16[512,2048]{1,0:T(8,128)(2,1)} fusion(f32[512,2048]{1,0:T(8,128)} %get-tuple-element.163, f32[512,2048]{1,0:T(8,128)} %get-tuple-element.178, bf16[1024,2048]{1,0:T(8,128)(2,1)} %maximum_select_fusion.3, bf16[1024,2048]{1,0:T(8,128)(2,1)} %collective-permute-done.25, pred[]{:T(512)S(6)} %eq.154, ...), kind=kOutput, calls=%fused_computation.36 | convolution fusion | flops 4356833280 | bytes 20971522 | tf_op jit(solution)/shard_map/dot_general | solution.py:55
  500.5 34.4 %collective-permute-done.30 = bf16[256,2048]{1,0:T(8,128)(2,1)} collective-permute-done((bf16[256,2048]{1,0:T(8,128)(2,1)S(1)}, bf16[256,2048]{1,0:T(8,128)(2,1)}, u32[]{:S(2)}, u32[]{:S(2)}) %collective-permute-start.30) | collective-permute-done | bytes 1048608 | tf_op jit(solution)/shard_map/ppermute | solution.py:15
  598.0 14.3 multiply_reduce_fusion
  612.3 15.9 %multiply_convert_fusion = bf16[4,512,2048]{2,1,0:T(8,128)(2,1)} fusion(f32[4,512,2048]{2,1,0:T(8,128)} %get-tuple-element.180, f32[4,512,2048]{2,1,0:T(8,128)} %get-tuple-element.177, f32[4,512]{1,0:T(4,128)S(1)} %get-tuple-element.179, f32[4,512]{1,0:T(4,128)S(1)} %log_add_fusion), kind=kLoop, calls=%fused_computation.2 | loop fusion | flops 16777216 | bytes 41959424 | tf_op jit(solution)/shard_map/while/body/eval_jaxpr/convert_element_type | solution.py:256
  650.4 121.4 %collective-permute-done.46 = bf16[256,2048]{1,0:T(8,128)(2,1)S(1)} collective-permute-done((bf16[256,2048]{1,0:T(8,128)(2,1)S(1)}, bf16[256,2048]{1,0:T(8,128)(2,1)S(1)}, u32[]{:S(2)}, u32[]{:S(2)}) %collective-permute-start.46) | collective-permute-done | bytes 1048608 | tf_op jit(solution)/shard_map/ppermute | solution.py:15
  772.7 21.6 %collective-permute-done.36 = bf16[1024,512]{0,1:T(8,128)(2,1)S(1)} collective-permute-done((bf16[1024,512]{0,1:T(8,128)(2,1)S(1)}, bf16[1024,512]{0,1:T(8,128)(2,1)S(1)}, u32[]{:S(2)}, u32[]{:S(2)}) %collective-permute-start.36) | collective-permute-done | bytes 1048608 | tf_op jit(solution)/shard_map/ppermute | solution.py:15
  794.3 12.9 collective-permute-start.47
  816.8 12.9 collective-permute-start.37
  894.5 18.2 %collective-permute-done.42 = bf16[2048,256]{1,0:T(8,128)(2,1)} collective-permute-done((bf16[2048,256]{1,0:T(8,128)(2,1)S(1)}, bf16[2048,256]{1,0:T(8,128)(2,1)}, u32[]{:S(2)}, u32[]{:S(2)}) %collective-permute-start.42) | collective-permute-done | bytes 1048608 | tf_op jit(solution)/shard_map/ppermute | solution.py:15
  915.3 34.9 %collective-permute-done.38 = bf16[256,6144]{1,0:T(8,128)(2,1)} collective-permute-done((bf16[256,6144]{1,0:T(8,128)(2,1)}, bf16[256,6144]{1,0:T(8,128)(2,1)}, u32[]{:S(2)}, u32[]{:S(2)}) %collective-permute-start.38) | collective-permute-done | bytes 3145760 | tf_op jit(solution)/shard_map/ppermute | solution.py:15
  973.5 24.9 %collective-permute-done.39 = bf16[128,6144]{1,0:T(8,128)(2,1)} collective-permute-done((bf16[128,6144]{1,0:T(8,128)(2,1)}, bf16[128,6144]{1,0:T(8,128)(2,1)}, u32[]{:S(2)}, u32[]{:S(2)}) %collective-permute-start.39) | collective-permute-done | bytes 1572896 | tf_op jit(solution)/shard_map/ppermute | solution.py:15
  1008.2 17.9 %fusion.113 = (f32[4,17]{1,0:T(4,128)S(1)}, f32[128,4,17]{2,1,0:T(4,128)S(1)}) fusion(bf16[17,128,2048]{2,1,0:T(8,128)(2,1)S(1)} %bitcast.136, f32[128,2048,4]{1,0,2:T(8,128)S(1)} %add_bitcast_fusion), kind=kOutput, calls=%fused_computation.270 | convolution fusion | flops 213918144 | bytes 13142288 | tf_op jit(solution)/shard_map/transpose(jvp(tkj,jtd->ktd))/dot_general | solution.py:35
  1056.6 16.9 %reduce-scatter.11.cloned.1.call-done = bf16[256,128]{1,0:T(8,128)(2,1)} async-done(((bf16[2048,128]{1,0:T(8,128)(2,1)}), bf16[256,128]{1,0:T(8,128)(2,1)}) %reduce-scatter.11.cloned.1.call-update) | async-done | bytes 65552 | tf_op jit(solution)/shard_map/reduce_scatter | solution.py:332
  1075.0 72.3 %reduce-scatter.9.cloned.1.call-done = bf16[256,128]{1,0:T(8,128)(2,1)} async-done(((bf16[2048,128]{1,0:T(8,128)(2,1)}), bf16[256,128]{1,0:T(8,128)(2,1)}) %reduce-scatter.9.cloned.1.call-update) | async-done | bytes 65552 | tf_op jit(solution)/shard_map/reduce_scatter | solution.py:329
  1153.4 78.7 %all-reduce.10.cloned.1.call-done = f32[2048,68]{0,1:T(8,128)} async-done(((f32[2048,68]{0,1:T(8,128)}), f32[2048,68]{0,1:T(8,128)}) %all-reduce.10.cloned.1.call-update) | async-done | bytes 557072 | tf_op jit(solution)/shard_map/psum | solution.py:310
  1232.1 25.5 %fusion = bf16[17,128,2048]{2,0,1:T(8,128)(2,1)} fusion(f32[1,128,2048]{2,0,1:T(1,128)S(1)} %broadcast_in_dim.111, f32[128,4,17]{2,1,0:T(4,128)S(1)} %copy-done.27, f32[128,2048,4]{1,0,2:T(8,128)} %copy-done.18), kind=kOutput, calls=%fused_computation.1 | convolution fusion | flops 222822400 | bytes 14190592 | tf_op jit(solution)/shard_map/transpose(jvp(tkj,jtd->ktd))/dot_general | solution.py:35
  1257.7 13.6 copy.76
  1271.6 31.9 %all-reduce.6 = (f32[2048]{0:T(1024)S(1)}, f32[68,68]{1,0:T(8,128)S(1)}, f32[68]{0:T(128)S(1)}, f32[2048]{0:T(1024)S(1)}, f32[2048]{0:T(1024)S(1)}, /*index=5*/f32[2048]{0:T(1024)S(1)}, f32[2048]{0:T(1024)S(1)}) all-reduce(f32[2048]{0:T(1024)S(1)} %get-tuple-element.133, ...), channel_id=1, replica_groups=mesh['dp'=8,'tensor'=16] {'dp'}, use_global_device_ids=true, to_apply=%region_17.18 | all-reduce | flops 14932 | bytes 119456 | tf_op jit(solution)/shard_map/psum | solution.py:310
  1303.6 63.0 %all-reduce.5 = (f32[2048]{0:T(1024)}, f32[68,68]{1,0:T(8,128)}, f32[68]{0:T(128)}, f32[2048]{0:T(1024)}, f32[2048]{0:T(1024)}, /*index=5*/f32[2048]{0:T(1024)}, f32[2048]{0:T(1024)}) all-reduce(f32[2048]{0:T(1024)S(1)} %get-tuple-element.154, f32[68,68]{1,0:T(8,128)S(1)} %get-tuple-element.155, ...), channel_id=1, replica_groups=mesh['dp'=8,'tensor'=16] {'tensor'}, use_global_device_ids=true, to_apply=%region_18.19 | all-reduce | flops 14932 | bytes 119456 | tf_op jit(solution)/shard_map/psum | solution.py:309
  1368.4 21.8 %reduce-scatter.17.cloned.1.call-done = bf16[512,256]{1,0:T(8,128)(2,1)} async-done(((bf16[512,2048]{1,0:T(8,128)(2,1)}), bf16[512,256]{1,0:T(8,128)(2,1)}) %reduce-scatter.17.cloned.1.call-update) | async-done | bytes 262160 | tf_op jit(solution)/shard_map/reduce_scatter | solution.py:341
  1392.0 116.1 %all-reduce.12.cloned.1.call-done = f32[2048,68]{0,1:T(8,128)} async-done(((f32[2048,68]{0,1:T(8,128)}), f32[2048,68]{0,1:T(8,128)}) %all-reduce.12.cloned.1.call-update) | async-done | bytes 557072 | tf_op jit(solution)/shard_map/psum | solution.py:309
  (452 shorter events, 406.8 us)
Async XLA Ops:
  7.2 1046.4 %reduce-scatter.13.cloned.1.call-start = ((), (), s32[]{:S(2)}) async-start(), calls=%async_computation.11 | async-start | bytes 589824 | tf_op jit(solution)/shard_map/reduce_scatter | solution.py:335
  7.2 68.0 %collective-permute-start.8 = (bf16[2048,128]{1,0:T(8,128)(2,1)}, bf16[2048,128]{1,0:T(8,128)(2,1)}, u32[]{:S(2)}, u32[]{:S(2)}) collective-permute-start(bf16[2048,128]{1,0:T(8,128)(2,1)} %param.28), channel_id=1, source_target_pairs={{0,1},{1,0},{2,3},{3,2},{4,5},{5,4},{6,7},{7,6},{8,9},{9,8},{10,11... | collective-permute-start | bytes 1572872 | tf_op jit(solution)/shard_map/ppermute | solution.py:15
  8.8 61.6 %collective-permute-start.2 = (bf16[2048,128]{1,0:T(8,128)(2,1)}, bf16[2048,128]{1,0:T(8,128)(2,1)}, u32[]{:S(2)}, u32[]{:S(2)}) collective-permute-start(bf16[2048,128]{1,0:T(8,128)(2,1)} %param.30), channel_id=1, source_target_pairs={{0,1},{1,0},{2,3},{3,2},{4,5},{5,4},{6,7},{7,6},{8,9},{9,8},{10,11... | collective-permute-start | bytes 1572872 | tf_op jit(solution)/shard_map/ppermute | solution.py:15
  49.0 52.7 %collective-permute-start.13 = (bf16[2048,256]{1,0:T(8,128)(2,1)}, bf16[2048,256]{1,0:T(8,128)(2,1)}, u32[]{:S(2)}, u32[]{:S(2)}) collective-permute-start(bf16[2048,256]{1,0:T(8,128)(2,1)} %maximum_select_fusion.29), channel_id=1, source_target_pairs={{0,2},{1,3},{2,0},{3,1},{4,6},{5,7},{6,4},{7,5},{8,10},{9,11},{10,... | collective-permute-start | bytes 3145736 | tf_op jit(solution)/shard_map/ppermute | solution.py:15
  75.3 47.7 %collective-permute-start.3 = (bf16[2048,256]{1,0:T(8,128)(2,1)S(1)}, bf16[2048,256]{1,0:T(8,128)(2,1)S(1)}, u32[]{:S(2)}, u32[]{:S(2)}) collective-permute-start(bf16[2048,256]{1,0:T(8,128)(2,1)S(1)} %maximum_select_fusion.23), channel_id=1, source_target_pairs={{0,2},{1,3},{2,0},{3,1},{4,6},{5,7},{6,4},{7,5},{8,10},{9,11},{10,... | collective-permute-start | bytes 3145736 | tf_op jit(solution)/shard_map/ppermute | solution.py:15
  77.6 67.8 %collective-permute-start.9 = (bf16[2048,256]{1,0:T(8,128)(2,1)S(1)}, bf16[2048,256]{1,0:T(8,128)(2,1)S(1)}, u32[]{:S(2)}, u32[]{:S(2)}) collective-permute-start(bf16[2048,256]{1,0:T(8,128)(2,1)S(1)} %maximum_select_fusion.27), channel_id=1, source_target_pairs={{0,2},{1,3},{2,0},{3,1},{4,6},{5,7},{6,4},{7,5},{8,10},{9,11},{10,... | collective-permute-start | bytes 3145736 | tf_op jit(solution)/shard_map/ppermute | solution.py:15
  124.4 102.2 %collective-permute-start.22 = (bf16[2048,512]{1,0:T(8,128)(2,1)}, bf16[2048,512]{1,0:T(8,128)(2,1)}, u32[]{:S(2)}, u32[]{:S(2)}) collective-permute-start(bf16[2048,512]{1,0:T(8,128)(2,1)} %param.32), channel_id=1, source_target_pairs={{0,1},{1,0},{2,3},{3,2},{4,5},{5,4},{6,7},{7,6},{8,9},{9,8},{10,11... | collective-permute-start | bytes 6291464 | tf_op jit(solution)/shard_map/ppermute | solution.py:15
  145.5 75.9 %collective-permute-start.17 = (bf16[256,2048]{1,0:T(8,128)(2,1)}, bf16[256,2048]{1,0:T(8,128)(2,1)}, u32[]{:S(2)}, u32[]{:S(2)}) collective-permute-start(bf16[256,2048]{1,0:T(8,128)(2,1)} %maximum_select_fusion.32), channel_id=1, source_target_pairs={{0,2},{1,3},{2,0},{3,1},{4,6},{5,7},{6,4},{7,5},{8,10},{9,11},{10,... | collective-permute-start | bytes 3145736 | tf_op jit(solution)/shard_map/ppermute | solution.py:15
  149.3 63.7 %collective-permute-start.5 = (bf16[1024,512]{0,1:T(8,128)(2,1)}, bf16[1024,512]{0,1:T(8,128)(2,1)}, u32[]{:S(2)}, u32[]{:S(2)}) collective-permute-start(bf16[1024,512]{0,1:T(8,128)(2,1)} %maximum_select_fusion.24), channel_id=1, source_target_pairs={{0,2},{1,3},{2,0},{3,1},{4,6},{5,7},{6,4},{7,5},{8,10},{9,11},{10,... | collective-permute-start | bytes 3145736 | tf_op jit(solution)/shard_map/ppermute | solution.py:15
  231.7 131.5 %collective-permute-start.23 = (bf16[2048,1024]{1,0:T(8,128)(2,1)S(1)}, bf16[2048,1024]{1,0:T(8,128)(2,1)S(1)}, u32[]{:S(2)}, u32[]{:S(2)}) collective-permute-start(bf16[2048,1024]{1,0:T(8,128)(2,1)S(1)} %maximum_select_fusion.2), channel_id=1, source_target_pairs={{0,2},{1,3},{2,0},{3,1},{4,6},{5,7},{6,4},{7,5},{8,10},{9,11},{10,... | collective-permute-start | bytes 12582920 | tf_op jit(solution)/shard_map/ppermute | solution.py:15
  249.7 84.6 %collective-permute-start.19 = (bf16[128,2048]{1,0:T(8,128)(2,1)S(1)}, bf16[128,2048]{1,0:T(8,128)(2,1)S(1)}, u32[]{:S(2)}, u32[]{:S(2)}) collective-permute-start(bf16[128,2048]{1,0:T(8,128)(2,1)S(1)} %select_convert_fusion.23), channel_id=1, source_target_pairs={{0,4},{1,5},{2,6},{3,7},{4,0},{5,1},{6,2},{7,3},{8,12},{9,13},{10,... | collective-permute-start | bytes 1572872 | tf_op jit(solution)/shard_map/ppermute | solution.py:15
  251.4 99.7 %collective-permute-start.24 = (bf16[512,2048]{1,0:T(8,128)(2,1)S(1)}, bf16[512,2048]{1,0:T(8,128)(2,1)S(1)}, u32[]{:S(2)}, u32[]{:S(2)}) collective-permute-start(bf16[512,2048]{1,0:T(8,128)(2,1)S(1)} %copy-done.25), channel_id=1, source_target_pairs={{0,1},{1,0},{2,3},{3,2},{4,5},{5,4},{6,7},{7,6},{8,9},{9,8},{10,11... | collective-permute-start | bytes 6291464 | tf_op jit(solution)/shard_map/ppermute | solution.py:15
  354.8 95.3 %collective-permute-start.25 = (bf16[1024,2048]{1,0:T(8,128)(2,1)}, bf16[1024,2048]{1,0:T(8,128)(2,1)}, u32[]{:S(2)}, u32[]{:S(2)}) collective-permute-start(bf16[1024,2048]{1,0:T(8,128)(2,1)} %maximum_select_fusion.3), channel_id=1, source_target_pairs={{0,2},{1,3},{2,0},{3,1},{4,6},{5,7},{6,4},{7,5},{8,10},{9,11},{10,... | collective-permute-start | bytes 12582920 | tf_op jit(solution)/shard_map/ppermute | solution.py:15
  491.7 47.9 %collective-permute-start.26 = (bf16[256,2048]{1,0:T(8,128)(2,1)S(1)}, bf16[256,2048]{1,0:T(8,128)(2,1)}, u32[]{:S(2)}, u32[]{:S(2)}) collective-permute-start(bf16[256,2048]{1,0:T(8,128)(2,1)S(1)} %select_convert_fusion.13), channel_id=1, source_target_pairs={{0,8},{1,9},{2,10},{3,11},{4,12},{5,13},{6,14},{7,15},{8,0},{9,1},... | collective-permute-start | bytes 3145736 | tf_op jit(solution)/shard_map/ppermute | solution.py:15
  564.8 281.5 %collective-permute-start.48 = (bf16[2048,1024]{1,0:T(8,128)(2,1)}, bf16[2048,1024]{1,0:T(8,128)(2,1)}, u32[]{:S(2)}, u32[]{:S(2)}) collective-permute-start(bf16[2048,1024]{1,0:T(8,128)(2,1)} %select_convert_fusion.1), channel_id=1, source_target_pairs={{0,2},{1,3},{2,0},{3,1},{4,6},{5,7},{6,4},{7,5},{8,10},{9,11},{10,... | collective-permute-start | bytes 12582920 | tf_op jit(solution)/shard_map/ppermute | solution.py:15
  587.6 448.6 %collective-permute-start.50 = (bf16[1024,2048]{1,0:T(8,128)(2,1)}, bf16[1024,2048]{1,0:T(8,128)(2,1)}, u32[]{:S(2)}, u32[]{:S(2)}) collective-permute-start(bf16[1024,2048]{1,0:T(8,128)(2,1)} %select_convert_fusion), channel_id=1, source_target_pairs={{0,2},{1,3},{2,0},{3,1},{4,6},{5,7},{6,4},{7,5},{8,10},{9,11},{10,... | collective-permute-start | bytes 12582920 | tf_op jit(solution)/shard_map/ppermute | solution.py:15
  641.2 130.6 %collective-permute-start.46 = (bf16[256,2048]{1,0:T(8,128)(2,1)S(1)}, bf16[256,2048]{1,0:T(8,128)(2,1)S(1)}, u32[]{:S(2)}, u32[]{:S(2)}) collective-permute-start(bf16[256,2048]{1,0:T(8,128)(2,1)S(1)} %select_convert_fusion.6), channel_id=1, source_target_pairs={{0,2},{1,3},{2,0},{3,1},{4,6},{5,7},{6,4},{7,5},{8,10},{9,11},{10,... | collective-permute-start | bytes 3145736 | tf_op jit(solution)/shard_map/ppermute | solution.py:15
  642.6 151.7 %collective-permute-start.36 = (bf16[1024,512]{0,1:T(8,128)(2,1)S(1)}, bf16[1024,512]{0,1:T(8,128)(2,1)S(1)}, u32[]{:S(2)}, u32[]{:S(2)}) collective-permute-start(bf16[1024,512]{0,1:T(8,128)(2,1)S(1)} %bitcast.146), channel_id=1, source_target_pairs={{0,2},{1,3},{2,0},{3,1},{4,6},{5,7},{6,4},{7,5},{8,10},{9,11},{10,... | collective-permute-start | bytes 3145736 | tf_op jit(solution)/shard_map/ppermute | solution.py:15
  643.2 173.5 %collective-permute-start.34 = (bf16[1024,512]{0,1:T(8,128)(2,1)S(1)}, bf16[1024,512]{0,1:T(8,128)(2,1)S(1)}, u32[]{:S(2)}, u32[]{:S(2)}) collective-permute-start(bf16[1024,512]{0,1:T(8,128)(2,1)S(1)} %bitcast.145), channel_id=1, source_target_pairs={{0,2},{1,3},{2,0},{3,1},{4,6},{5,7},{6,4},{7,5},{8,10},{9,11},{10,... | collective-permute-start | bytes 3145736 | tf_op jit(solution)/shard_map/ppermute | solution.py:15
  771.8 67.4 %collective-permute-start.40 = (bf16[2048,256]{1,0:T(8,128)(2,1)S(1)}, bf16[2048,256]{1,0:T(8,128)(2,1)S(1)}, u32[]{:S(2)}, u32[]{:S(2)}) collective-permute-start(bf16[2048,256]{1,0:T(8,128)(2,1)S(1)} %select_convert_fusion.9), channel_id=1, source_target_pairs={{0,2},{1,3},{2,0},{3,1},{4,6},{5,7},{6,4},{7,5},{8,10},{9,11},{10,... | collective-permute-start | bytes 3145736 | tf_op jit(solution)/shard_map/ppermute | solution.py:15
  794.3 59.6 %collective-permute-start.47 = (bf16[128,2048]{1,0:T(8,128)(2,1)S(1)}, bf16[128,2048]{1,0:T(8,128)(2,1)}, u32[]{:S(2)}, u32[]{:S(2)}) collective-permute-start(bf16[128,2048]{1,0:T(8,128)(2,1)S(1)} %select_convert_fusion.15), channel_id=1, source_target_pairs={{0,1},{1,0},{2,3},{3,2},{4,5},{5,4},{6,7},{7,6},{8,9},{9,8},{10,11... | collective-permute-start | bytes 1572872 | tf_op jit(solution)/shard_map/ppermute | solution.py:15
  855.9 199.2 %reduce-scatter.7.cloned.1.call-start = ((), (), s32[]{:S(2)}) async-start(), calls=%async_computation.8 | async-start | bytes 589824 | tf_op jit(solution)/shard_map/reduce_scatter | solution.py:326
  877.2 73.0 %collective-permute-start.38 = (bf16[256,6144]{1,0:T(8,128)(2,1)}, bf16[256,6144]{1,0:T(8,128)(2,1)}, u32[]{:S(2)}, u32[]{:S(2)}) collective-permute-start(bf16[256,6144]{1,0:T(8,128)(2,1)} %select_convert_fusion.2), channel_id=1, source_target_pairs={{0,8},{1,9},{2,10},{3,11},{4,12},{5,13},{6,14},{7,15},{8,0},{9,1},... | collective-permute-start | bytes 9437192 | tf_op jit(solution)/shard_map/ppermute | solution.py:15
  888.9 184.6 %reduce-scatter.11.cloned.1.call-start = ((), (), s32[]{:S(2)}) async-start(), calls=%async_computation.10 | async-start | bytes 589824 | tf_op jit(solution)/shard_map/reduce_scatter | solution.py:332
  893.3 70.4 %collective-permute-start.45 = (bf16[2048,128]{1,0:T(8,128)(2,1)S(1)}, bf16[2048,128]{1,0:T(8,128)(2,1)S(1)}, u32[]{:S(2)}, u32[]{:S(2)}) collective-permute-start(bf16[2048,128]{1,0:T(8,128)(2,1)S(1)} %select_convert_fusion.16), channel_id=1, source_target_pairs={{0,1},{1,0},{2,3},{3,2},{4,5},{5,4},{6,7},{7,6},{8,9},{9,8},{10,11... | collective-permute-start | bytes 1572872 | tf_op jit(solution)/shard_map/ppermute | solution.py:15
  914.5 56.4 %collective-permute-start.43 = (bf16[2048,128]{1,0:T(8,128)(2,1)S(1)}, bf16[2048,128]{1,0:T(8,128)(2,1)}, u32[]{:S(2)}, u32[]{:S(2)}) collective-permute-start(bf16[2048,128]{1,0:T(8,128)(2,1)S(1)} %select_convert_fusion.17), channel_id=1, source_target_pairs={{0,1},{1,0},{2,3},{3,2},{4,5},{5,4},{6,7},{7,6},{8,9},{9,8},{10,11... | collective-permute-start | bytes 1572872 | tf_op jit(solution)/shard_map/ppermute | solution.py:15
  964.7 182.7 %reduce-scatter.9.cloned.1.call-start = ((), (), s32[]{:S(2)}) async-start(), calls=%async_computation.9 | async-start | bytes 589824 | tf_op jit(solution)/shard_map/reduce_scatter | solution.py:329
  969.9 59.5 %collective-permute-start.49 = (bf16[2048,512]{1,0:T(8,128)(2,1)}, bf16[2048,512]{1,0:T(8,128)(2,1)}, u32[]{:S(2)}, u32[]{:S(2)}) collective-permute-start(bf16[2048,512]{1,0:T(8,128)(2,1)} %select_convert_fusion.4), channel_id=1, source_target_pairs={{0,1},{1,0},{2,3},{3,2},{4,5},{5,4},{6,7},{7,6},{8,9},{9,8},{10,11... | collective-permute-start | bytes 6291464 | tf_op jit(solution)/shard_map/ppermute | solution.py:15
  973.0 259.1 %all-reduce.10.cloned.1.call-start = ((), (), s32[]{:S(2)}) async-start(), calls=%async_computation.6 | async-start | bytes 1179648 | tf_op jit(solution)/shard_map/psum | solution.py:310
  1029.4 337.2 %reduce-scatter.15.cloned.1.call-start = ((), (), s32[]{:S(2)}) async-start(), calls=%async_computation.12 | async-start | bytes 2359296 | tf_op jit(solution)/shard_map/reduce_scatter | solution.py:338
  1036.1 354.1 %reduce-scatter.17.cloned.1.call-start = ((), (), s32[]{:S(2)}) async-start(), calls=%async_computation.13 | async-start | bytes 2359296 | tf_op jit(solution)/shard_map/reduce_scatter | solution.py:341
  1053.5 454.5 %all-reduce.12.cloned.1.call-start = ((), (), s32[]{:S(2)}) async-start(), calls=%async_computation.7 | async-start | bytes 1179648 | tf_op jit(solution)/shard_map/psum | solution.py:309
  (129 other events, 2563.6 us)
Sparse Core Ops, SparseCore 0:
  856.0 71.1 reduce-scatter.12
  931.8 69.1 reduce-scatter.6
  1004.5 68.9 reduce-scatter.10
  1077.9 69.4 reduce-scatter.8
  1150.3 81.7 all-reduce.9
  1235.6 76.8 reduce-scatter.14
  1316.3 73.8 reduce-scatter.16
  1392.7 115.3 all-reduce.11
